TPU v7x, 32 devices: a whole 2x2x4 slice. The times are simulated.
32 devices in a mesh: win: 4 (over y, x), row: 2 (over core), col: 4 (over z).
Axes of the slice: x: 2, y: 2, z: 4, core: 2. Of those that a mesh axis runs over, the one named last changes fastest.
Arguments:
- spectra: bfloat16 [2, 8, 6144, 768], P(None, None, ('row', 'col'), 'win'), may hold values from -6 to 6
- gain: float32 [6144], P(('row', 'col')), may hold values from 0.1 to 3
Outputs:
- cross: float32 [2, 8, 6144, 6144], P(None, 'win', 'row', 'col')
All inputs are finite; a program needn't handle non-finite values.
Results may differ from a plain program's by a relative error of at most 0.0038.
Values may be sent and summed in bfloat16 or wider, within the bound.
A program may use at most 256 MiB of HBM per device.

v0:
```python
import jax
import jax.numpy as jnp
from jax import lax
from jax.sharding import PartitionSpec as P


def broadcast(value, axis, source):
    kept = jnp.where(lax.axis_index(axis) == source, value, 0).astype(value.dtype)
    return lax.psum(kept, axis)


def per_device(spectra, gain):
    calibrated = spectra.astype(jnp.float32) * gain[None, None, :, None]
    level = jnp.sqrt(jnp.mean(calibrated * calibrated, axis=(0, 1)))
    white = (calibrated / jnp.maximum(level, 0.5)).astype(jnp.bfloat16)
    regrouped = lax.all_to_all(white, "win", split_axis=1, concat_axis=3, tiled=True)
    windows = regrouped.shape[3]
    rows_block = lax.all_gather(regrouped, "col", axis=2, tiled=True)
    ratio = lax.axis_size("col") // lax.axis_size("row")
    col_width = rows_block.shape[2] // ratio
    col_index = lax.axis_index("col")
    portion = col_index % ratio
    root_row = col_index // ratio
    relayed = broadcast(rows_block, "row", root_row)
    cols_block = lax.dynamic_slice_in_dim(relayed, portion * col_width, col_width, 2)
    left_side = jnp.concatenate([rows_block[0], rows_block[1]], axis=-1)
    right_real = jnp.concatenate([cols_block[0], cols_block[1]], axis=-1)
    right_imag = jnp.concatenate([-cols_block[1], cols_block[0]], axis=-1)
    right_both = jnp.stack([right_real, right_imag])
    stacked = jnp.einsum(
        "fiw,ofjw->ofij", left_side, right_both, preferred_element_type=jnp.float32
    )
    return stacked / jnp.float32(windows)


def solution(mesh):
    in_specs = (P(None, None, ("row", "col"), "win"), P(("row", "col")))
    out_specs = P(None, "win", "row", "col")
    return jax.shard_map(
        per_device, mesh=mesh, in_specs=in_specs, out_specs=out_specs, check_vma=False
    )
```

profile of v0, /device:TPU:0, one launch (start us, length us, event | category | flops | bytes accessed | tf_op | source)
XLA Modules:
  0.0 643.1 jit_solution(993827543162699644)
XLA Ops:
  6.5 0.0 all-gather.2.cloned.1.call-start
  6.5 0.0 copy-start
  6.5 3.8 multiply_reduce_fusion
  10.3 0.2 sqrt_maximum_fusion
  10.5 0.0 copy-done
  10.5 1.9 divide_convert_fusion
  12.5 58.4 %all_to_all.18 = bf16[2,8,768,192]{2,3,0,1:T(8,128)(2,1)S(1)} all-to-all(bf16[2,8,768,192]{2,3,0,1:T(8,128)(2,1)S(1)} %divide_convert_fusion), channel_id=1, replica_groups=mesh['win'=4,'row'=2,'col'=4] {'win'}, dimensions={1} | all-to-all | bytes 9437184 | tf_op jit(solution)/shard_map/all_to_all | solution.py:16
  70.9 2.6 copy.15
  73.5 6.7 %copy.16 = bf16[2,2,768,768]{3,2,1,0:T(8,128)(2,1)} copy(bf16[2,2,768,768]{2,3,1,0:T(8,128)(2,1)} %bitcast.30) | data formatting | bytes 9437184 | tf_op jit(solution)/shard_map/all_to_all | solution.py:16
  80.2 0.0 all-gather.2.cloned.1.call-update
  80.2 0.2 all-reduce.2.cloned.1.call-start
  80.5 321.8 %all-gather.2.cloned.1.call-done = bf16[2,2,3072,768]{3,2,1,0:T(8,128)(2,1)} async-done(((bf16[2,2,768,768]{3,2,1,0:T(8,128)(2,1)}), bf16[2,2,3072,768]{3,2,1,0:T(8,128)(2,1)}) %all-gather.2.cloned.1.call-update) | async-done | bytes 18874384 | tf_op jit(solution)/shard_map/all_gather | solution.py:18
  402.2 16.7 %broadcast_select_fusion = bf16[2,2,3072,768]{3,2,1,0:T(8,128)(2,1)} fusion(bf16[2,2,3072,768]{3,2,1,0:T(8,128)(2,1)} %all-gather.2.cloned.1.call-done, pred[]{:T(512)S(6)} %eq.5), kind=kLoop, calls=%fused_computation.6 | loop fusion | flops 9437184 | bytes 37748736 | tf_op jit(solution)/shard_map/jit(_where)/select_n | solution.py:8
  418.9 0.0 all-reduce.2.cloned.1.call-update
  418.9 16.4 %slice_bitcast_fusion.1 = (bf16[2,3072,768]{2,1,0:T(8,128)(2,1)}, bf16[2,3072,768]{2,1,0:T(8,128)(2,1)}) fusion(bf16[2,2,3072,768]{3,2,1,0:T(8,128)(2,1)} %all-gather.2.cloned.1.call-done), kind=kLoop, calls=%fused_computation.8 | loop fusion | bytes 37748736 | tf_op jit(solution)/shard_map/squeeze | solution.py:26
  435.3 45.7 %all-reduce.2.cloned.1.call-done = bf16[2,2,3072,768]{3,2,1,0:T(8,128)(2,1)} async-done(((bf16[2,2,3072,768]{3,2,1,0:T(8,128)(2,1)}), bf16[2,2,3072,768]{3,2,1,0:T(8,128)(2,1)}) %all-reduce.2.cloned.1.call-update) | async-done | bytes 18874384 | tf_op jit(solution)/shard_map/psum | solution.py:9
  481.0 2.6 dynamic-slice_bitcast_fusion.1
  483.6 3.6 fusion.4
  487.2 7.0 %maximum_bitcast_fusion.2 = (bf16[1,2,1536,1536]{3,2,1,0:T(8,128)(2,1)}, bf16[1,2,1536,1536]{3,2,1,0:T(8,128)(2,1)}) fusion(bf16[2,1536,768]{2,1,0:T(8,128)(2,1)S(1)} %get-tuple-element.6, bf16[2,1536,768]{2,1,0:T(8,128)(2,1)S(1)} %dynamic-slice_bitcast_fusion.1, bf16[2,1536,768]{2,1,0:T(8,128)(2,1)S(1)} %get-tuple-element.5), kind=kLoop, calls=%fused_computation.9 | loop fusion | flops 37748736 | bytes 33030144 | tf_op jit(solution)/shard_map/stack | solution.py:29
  494.2 69.0 %multiply_bitcast_fusion = f32[2,2,3072,1536]{2,3,0,1:T(8,128)} fusion(bf16[2,3072,768]{2,1,0:T(8,128)(2,1)} %get-tuple-element.8, bf16[2,3072,768]{2,1,0:T(8,128)(2,1)} %get-tuple-element.7, bf16[1,2,1536,1536]{3,2,1,0:T(8,128)(2,1)} %get-tuple-element.10, bf16[1,2,1536,1536]{3,2,1,0:T(8,128)(2,1)} %get-tuple-element.9), kind=kOutput, calls=%fused_computation | convolution fusion | flops 58048118784 | bytes 113246208 | tf_op jit(solution)/shard_map/fiw,ofjw->ofij/dot_general | solution.py:30
  563.2 73.1 %copy.18 = f32[2,2,3072,1536]{3,2,1,0:T(8,128)} copy(f32[2,2,3072,1536]{2,3,0,1:T(8,128)} %multiply_bitcast_fusion) | data formatting | bytes 150994944 | tf_op jit(solution)/shard_map/div | solution.py:33
Async XLA Ops:
  6.5 395.7 %all-gather.2.cloned.1.call-start = ((), (), s32[]{:S(2)}) async-start(), calls=%async_computation.1 | async-start | bytes 23592960 | tf_op jit(solution)/shard_map/all_gather | solution.py:18
  6.5 4.0 copy-start
  80.2 400.8 %all-reduce.2.cloned.1.call-start = ((), (), s32[]{:S(2)}) async-start(), calls=%async_computation.2 | async-start | bytes 37748736 | tf_op jit(solution)/shard_map/psum | solution.py:9
Sparse Core Ops, SparseCore 0:
  80.3 321.8 all-gather.1
  419.1 61.8 all-reduce.1
where the time goes:
time: 645 us; the launch traced here: 643 us
  waiting for transfers between devices  367 us (57%)
  local copies, waits for them, and re-layouts  101 us (16%)
  matrix products  69 us (11%)
  blocking collectives  58.4 us (9%)
  other arithmetic  33.1 us (5%)
  between operations  13.5 us (2%)
    all_gather x1, waiting for transfers between devices, per_device(): rows_block = lax.all_gather(regrouped, 'col', axis=2, tiled=True)  322 us
    div x1, local copies, waits for them, and re-layouts, per_device(): return stacked / jnp.float32(windows)  73.1 us
    dot_general x1, matrix products, per_device(): jnp.einsum('fiw,ofjw->ofij', left_side, right_both, preferred_element_typ...  69 us
    all_to_all x1, blocking collectives, per_device(): lax.all_to_all(white, 'win', split_axis=1, concat_axis=3, tiled=True)  58.4 us
    psum x1, waiting for transfers between devices, broadcast(): return lax.psum(kept, axis)  45.7 us
    select_n x1, other arithmetic, broadcast(): jnp.where(lax.axis_index(axis) == source, value, 0).astype(value.dtype)  16.7 us
    squeeze x1, local copies, waits for them, and re-layouts, per_device(): left_side = jnp.concatenate([rows_block[0], rows_block[1]], axis=-1)  16.4 us
  transfers between devices with their start and end apart: 2, of which 2 were waited for; matrix products, arithmetic and copies ran while one was open for 3% of the time, Pallas kernels for 0%

commit v1 on v0

--- a/solution.py
+++ b/solution.py
@@ -15,7 +15,25 @@
     white = (calibrated / jnp.maximum(level, 0.5)).astype(jnp.bfloat16)
     regrouped = lax.all_to_all(white, "win", split_axis=1, concat_axis=3, tiled=True)
     windows = regrouped.shape[3]
-    rows_block = lax.all_gather(regrouped, "col", axis=2, tiled=True)
+    all_rows = jax.lax.axis_index("col")
+    v_next = jax.lax.axis_size("col")
+    found_now, before, b_now = (v_next, all_rows, regrouped.shape[2])
+    store = tuple((nth * found_now if t == 2 else nth for t, nth in enumerate(regrouped.shape)))
+    piece_out = jnp.zeros(store, regrouped.dtype)
+    field_out = e_next = regrouped
+    rows_block = lax.dynamic_update_slice_in_dim(piece_out, regrouped, before * b_now, axis=2)
+    for j in range(1, found_now // 2 + 1):
+        s_next = tuple(((t, (t + 1) % found_now) for t in range(found_now)))
+        field_out = jax.lax.ppermute(field_out, "col", s_next)
+        rows_block = lax.dynamic_update_slice_in_dim(
+            rows_block, field_out, (before - j) % found_now * b_now, axis=2
+        )
+        if 2 * j < found_now:
+            last = tuple(((t, (t - 1) % found_now) for t in range(found_now)))
+            e_next = jax.lax.ppermute(e_next, "col", last)
+            rows_block = lax.dynamic_update_slice_in_dim(
+                rows_block, e_next, (before + j) % found_now * b_now, axis=2
+            )
     ratio = lax.axis_size("col") // lax.axis_size("row")
     col_width = rows_block.shape[2] // ratio
     col_index = lax.axis_index("col")

time: 645 us -> 630 us (0.977)
  waiting for transfers between devices: 367 us -> 243 us
  starting transfers between devices: 0.22 us -> 100 us
  local copies, waits for them, and re-layouts: 101 us -> 120 us
  other arithmetic: 33.1 us -> 24.2 us
    all_gather x1 -> x0, waiting for transfers between devices: 322 us -> none  [per_device(): rows_block = lax.all_gather(regrouped, 'col', axis=2, tiled=True)]
    ppermute x0 -> x3, waiting for transfers between devices: none -> 198 us  [the longest x2 198 us: per_device(): field_out = jax.lax.ppermute(field_out, 'col', s_next)]
    ppermute x0 -> x3, starting transfers between devices: none -> 100 us  [the longest x2 98 us: per_device(): field_out = jax.lax.ppermute(field_out, 'col', s_next)]
    dynamic_update_slice x0 -> x4, local copies, waits for them, and re-layouts: none -> 9.23 us  [the longest x2 5.78 us: per_device(): lax.dynamic_update_slice_in_dim(rows_block, field_out, (before - j) % fou...]
    select_n x1, other arithmetic: 16.7 us -> 7.73 us  [broadcast(): jnp.where(lax.axis_index(axis) == source, value, 0).astype(value.dtype)]
    unnamed x2 -> x6, local copies, waits for them, and re-layouts: 0.01 us -> 7.83 us
  transfers between devices with their start and end apart: 2 -> 4, of which waited for: 2 -> 3; matrix products, arithmetic and copies ran while one was open for 3% -> 4% of each run, Pallas kernels for 0% -> 0%
where the time goes in v1:
time: 630 us; the launch traced here: 628 us
  waiting for transfers between devices  243 us (39%)
  local copies, waits for them, and re-layouts  120 us (19%)
  starting transfers between devices  100 us (16%)
  matrix products  68.9 us (11%)
  blocking collectives  58.4 us (9%)
  other arithmetic  24.2 us (4%)
  between operations  13.5 us (2%)
    ppermute x2, waiting for transfers between devices, per_device(): field_out = jax.lax.ppermute(field_out, 'col', s_next)  198 us
    ppermute x2, starting transfers between devices, per_device(): field_out = jax.lax.ppermute(field_out, 'col', s_next)  98 us
    div x1, local copies, waits for them, and re-layouts, per_device(): return stacked / jnp.float32(windows)  73.1 us
    dot_general x1, matrix products, per_device(): jnp.einsum('fiw,ofjw->ofij', left_side, right_both, preferred_element_typ...  68.9 us
    all_to_all x1, blocking collectives, per_device(): lax.all_to_all(white, 'win', split_axis=1, concat_axis=3, tiled=True)  58.4 us
    psum x1, waiting for transfers between devices, broadcast(): return lax.psum(kept, axis)  45.7 us
    squeeze x1, local copies, waits for them, and re-layouts, per_device(): left_side = jnp.concatenate([rows_block[0], rows_block[1]], axis=-1)  16.3 us
  transfers between devices with their start and end apart: 4, of which 3 were waited for; matrix products, arithmetic and copies ran while one was open for 4% of the time, Pallas kernels for 0%

profile of v1, /device:TPU:0, one launch (start us, length us, event | category | flops | bytes accessed | tf_op | source)
XLA Modules:
  0.0 628.1 jit_solution(16865635126119434472)
XLA Ops:
  6.5 0.0 all-reduce.2.cloned.1.call-start
  6.5 0.0 copy-start.1
  6.5 3.8 multiply_reduce_fusion
  10.3 0.2 sqrt_maximum_fusion
  10.5 0.0 copy-done.1
  10.5 1.9 divide_convert_fusion
  12.5 58.4 %all_to_all.18 = bf16[2,8,768,192]{2,3,0,1:T(8,128)(2,1)S(1)} all-to-all(bf16[2,8,768,192]{2,3,0,1:T(8,128)(2,1)S(1)} %divide_convert_fusion), channel_id=1, replica_groups=mesh['win'=4,'row'=2,'col'=4] {'win'}, dimensions={1} | all-to-all | bytes 9437184 | tf_op jit(solution)/shard_map/all_to_all | solution.py:16
  70.9 2.6 copy.19
  73.5 6.7 %copy.20 = bf16[2,2,768,768]{3,2,1,0:T(8,128)(2,1)} copy(bf16[2,2,768,768]{2,3,1,0:T(8,128)(2,1)} %bitcast.30) | data formatting | bytes 9437184 | tf_op jit(solution)/shard_map/all_to_all | solution.py:16
  80.2 1.6 collective-permute-start
  81.7 2.2 collective-permute-start.1
  84.0 103.0 %collective-permute-done = bf16[2,2,768,768]{3,2,1,0:T(8,128)(2,1)} collective-permute-done((bf16[2,2,768,768]{3,2,1,0:T(8,128)(2,1)}, bf16[2,2,768,768]{3,2,1,0:T(8,128)(2,1)}, u32[]{:S(2)}, u32[]{:S(2)}) %collective-permute-start) | collective-permute-done | bytes 4718624 | tf_op jit(solution)/shard_map/ppermute | solution.py:27
  187.0 96.4 %collective-permute-start.2 = (bf16[2,2,768,768]{3,2,1,0:T(8,128)(2,1)}, bf16[2,2,768,768]{3,2,1,0:T(8,128)(2,1)}, u32[]{:S(2)}, u32[]{:S(2)}) collective-permute-start(bf16[2,2,768,768]{3,2,1,0:T(8,128)(2,1)} %collective-permute-done), channel_id=1, source_target_pairs={{0,1},{1,2},{2,3},{3,0},{4,5},{5,6},{6,7},{7,4},{8,9},{9,10},{10,1... | collective-permute-start | bytes 14155784 | tf_op jit(solution)/shard_map/ppermute | solution.py:27
  283.4 0.0 copy-start.2
  283.4 1.3 broadcast_in_dim.3
  284.8 1.0 copy-done.2
  285.8 0.6 constant_dynamic-update-slice_fusion.3
  286.3 2.9 constant_dynamic-update-slice_fusion.2
  289.2 0.0 collective-permute-done.1
  289.2 2.9 constant_dynamic-update-slice_fusion.1
  292.1 94.5 %collective-permute-done.2 = bf16[2,2,768,768]{3,2,1,0:T(8,128)(2,1)} collective-permute-done((bf16[2,2,768,768]{3,2,1,0:T(8,128)(2,1)}, bf16[2,2,768,768]{3,2,1,0:T(8,128)(2,1)}, u32[]{:S(2)}, u32[]{:S(2)}) %collective-permute-start.2) | collective-permute-done | bytes 4718624 | tf_op jit(solution)/shard_map/ppermute | solution.py:27
  386.6 2.9 constant_dynamic-update-slice_fusion
  389.5 0.0 copy-start
  389.5 6.8 %copy-done = bf16[2,2,3072,768]{3,2,1,0:T(8,128)(2,1)} copy-done((bf16[2,2,3072,768]{3,2,1,0:T(8,128)(2,1)}, bf16[2,2,3072,768]{3,2,1,0:T(8,128)(2,1)S(1)}, u32[]{:S(2)}) %copy-start) | copy-done | bytes 18874392
  396.4 7.7 %broadcast_select_fusion = bf16[2,2,3072,768]{3,2,1,0:T(8,128)(2,1)} fusion(bf16[2,2,3072,768]{3,2,1,0:T(8,128)(2,1)S(1)} %constant_dynamic-update-slice_fusion, pred[]{:T(512)S(6)} %eq.8), kind=kLoop, calls=%fused_computation.6 | loop fusion | flops 9437184 | bytes 37748736 | tf_op jit(solution)/shard_map/jit(_where)/select_n | solution.py:8
  404.1 0.0 all-reduce.2.cloned.1.call-update
  404.1 16.3 %slice_bitcast_fusion.1 = (bf16[2,3072,768]{2,1,0:T(8,128)(2,1)}, bf16[2,3072,768]{2,1,0:T(8,128)(2,1)}) fusion(bf16[2,2,3072,768]{3,2,1,0:T(8,128)(2,1)} %copy-done), kind=kLoop, calls=%fused_computation.8 | loop fusion | bytes 37748736 | tf_op jit(solution)/shard_map/squeeze | solution.py:44
  420.5 45.7 %all-reduce.2.cloned.1.call-done = bf16[2,2,3072,768]{3,2,1,0:T(8,128)(2,1)} async-done(((bf16[2,2,3072,768]{3,2,1,0:T(8,128)(2,1)}), bf16[2,2,3072,768]{3,2,1,0:T(8,128)(2,1)}) %all-reduce.2.cloned.1.call-update) | async-done | bytes 18874384 | tf_op jit(solution)/shard_map/psum | solution.py:9
  466.2 2.6 dynamic-slice_bitcast_fusion.1
  468.8 3.6 fusion.4
  472.4 6.9 %maximum_bitcast_fusion.2 = (bf16[1,2,1536,1536]{3,2,1,0:T(8,128)(2,1)}, bf16[1,2,1536,1536]{3,2,1,0:T(8,128)(2,1)}) fusion(bf16[2,1536,768]{2,1,0:T(8,128)(2,1)S(1)} %get-tuple-element.6, bf16[2,1536,768]{2,1,0:T(8,128)(2,1)S(1)} %dynamic-slice_bitcast_fusion.1, bf16[2,1536,768]{2,1,0:T(8,128)(2,1)S(1)} %get-tuple-element.5), kind=kLoop, calls=%fused_computation.9 | loop fusion | flops 37748736 | bytes 33030144 | tf_op jit(solution)/shard_map/stack | solution.py:47
  479.4 68.9 %multiply_bitcast_fusion = f32[2,2,3072,1536]{2,3,0,1:T(8,128)} fusion(bf16[2,3072,768]{2,1,0:T(8,128)(2,1)} %get-tuple-element.8, bf16[2,3072,768]{2,1,0:T(8,128)(2,1)} %get-tuple-element.7, bf16[1,2,1536,1536]{3,2,1,0:T(8,128)(2,1)} %get-tuple-element.10, bf16[1,2,1536,1536]{3,2,1,0:T(8,128)(2,1)} %get-tuple-element.9), kind=kOutput, calls=%fused_computation | convolution fusion | flops 58048118784 | bytes 113246208 | tf_op jit(solution)/shard_map/fiw,ofjw->ofij/dot_general | solution.py:48
  548.2 73.1 %copy.24 = f32[2,2,3072,1536]{3,2,1,0:T(8,128)} copy(f32[2,2,3072,1536]{2,3,0,1:T(8,128)} %multiply_bitcast_fusion) | data formatting | bytes 150994944 | tf_op jit(solution)/shard_map/div | solution.py:51
Async XLA Ops:
  6.5 459.6 %all-reduce.2.cloned.1.call-start = ((), (), s32[]{:S(2)}) async-start(), calls=%async_computation.1 | async-start | bytes 37748736 | tf_op jit(solution)/shard_map/psum | solution.py:9
  6.5 4.0 copy-start.1
  80.2 106.9 %collective-permute-start = (bf16[2,2,768,768]{3,2,1,0:T(8,128)(2,1)}, bf16[2,2,768,768]{3,2,1,0:T(8,128)(2,1)}, u32[]{:S(2)}, u32[]{:S(2)}) collective-permute-start(bf16[2,2,768,768]{3,2,1,0:T(8,128)(2,1)} %copy.20), channel_id=1, source_target_pairs={{0,1},{1,2},{2,3},{3,0},{4,5},{5,6},{6,7},{7,4},{8,9},{9,10},{10,1... | collective-permute-start | bytes 14155784 | tf_op jit(solution)/shard_map/ppermute | solution.py:27
  81.7 207.5 %collective-permute-start.1 = (bf16[2,2,768,768]{3,2,1,0:T(8,128)(2,1)}, bf16[2,2,768,768]{3,2,1,0:T(8,128)(2,1)}, u32[]{:S(2)}, u32[]{:S(2)}) collective-permute-start(bf16[2,2,768,768]{3,2,1,0:T(8,128)(2,1)} %copy.20), channel_id=1, source_target_pairs={{0,3},{1,0},{2,1},{3,2},{4,7},{5,4},{6,5},{7,6},{8,11},{9,8},{10,9... | collective-permute-start | bytes 14155784 | tf_op jit(solution)/shard_map/ppermute | solution.py:33
  187.0 199.6 %collective-permute-start.2 = (bf16[2,2,768,768]{3,2,1,0:T(8,128)(2,1)}, bf16[2,2,768,768]{3,2,1,0:T(8,128)(2,1)}, u32[]{:S(2)}, u32[]{:S(2)}) collective-permute-start(bf16[2,2,768,768]{3,2,1,0:T(8,128)(2,1)} %collective-permute-done), channel_id=1, source_target_pairs={{0,1},{1,2},{2,3},{3,0},{4,5},{5,6},{6,7},{7,4},{8,9},{9,10},{10,1... | collective-permute-start | bytes 14155784 | tf_op jit(solution)/shard_map/ppermute | solution.py:27
  283.4 2.3 copy-start.2
  389.5 6.9 %copy-start = (bf16[2,2,3072,768]{3,2,1,0:T(8,128)(2,1)}, bf16[2,2,3072,768]{3,2,1,0:T(8,128)(2,1)S(1)}, u32[]{:S(2)}) copy-start(bf16[2,2,3072,768]{3,2,1,0:T(8,128)(2,1)S(1)} %constant_dynamic-update-slice_fusion) | copy-start | bytes 56623108
Sparse Core Ops, SparseCore 0:
  404.2 61.8 all-reduce.1
